TPU v7x, 256 devices: a whole 4x4x8 slice. The times are simulated.
256 devices in a mesh: cfg: 2 (over x_lo), seq: 128 (over y, z, x_hi, core).
Axes of the slice: x: 4 (x_hi: 2, x_lo: 2; x = x_hi * 2 + x_lo), y: 4, z: 8, core: 2. Of those that a mesh axis runs over, the one named last changes fastest.
Arguments:
- coarse_hidden: bfloat16 [2, 256, 64, 2048], P('cfg', 'seq'), may hold values from -6 to 6
- coarse_modulation: float32 [2, 2, 2048], P('cfg'), may hold values from -3 to 3
- final_weight: bfloat16 [2048, 32], replicated, may hold values from -0.125 to 0.125
- coarse_latent: float32 [256, 2048], P('seq'), may hold values from -6 to 6
- step_index: int32 [1], replicated, may hold values from 0 to 49
- guide_index: int32 [1], replicated, may hold values from 0 to 4095
- guide_scales: float32 [4096], replicated, may hold values from 1.5 to 6
- upsample_weight: float32 [288, 32], replicated, may hold values from -0.375 to 0.375
- upsample_bias: float32 [32], replicated, may hold values from -3 to 3
- embed_weight: bfloat16 [32, 2048], replicated, may hold values from -1 to 1
- embed_bias: float32 [2048], replicated, may hold values from -3 to 3
- fine_modulation: float32 [3, 2048], replicated, may hold values from -3 to 3
- project_weight: bfloat16 [2048, 3072], P(('cfg', 'seq')), may hold values from -0.125 to 0.125
- query_gain: float32 [128], replicated, may hold values from 0.25 to 1.75
- key_gain: float32 [128], replicated, may hold values from 0.25 to 1.75
- text_keys: bfloat16 [256, 1024], replicated, may hold values from -6 to 6
- text_values: bfloat16 [256, 1024], replicated, may hold values from -6 to 6
- text_length: int32 [1], replicated, may hold values from 192 to 256
- output_weight: bfloat16 [1024, 2048], P(None, ('cfg', 'seq')), may hold values from -0.1875 to 0.1875
Outputs:
- guided_velocity: float32 [256, 2048], P('seq')
- fine_latent: float32 [256, 2, 4096], P('seq', 'cfg')
- fine_hidden: bfloat16 [256, 2, 128, 2048], P('seq', 'cfg')
All inputs are finite; a program needn't handle non-finite values.
Results may differ from a plain program's by a relative error of at most 0.0053.
Values may be sent and summed in bfloat16 or wider, within the bound.
A program may use at most 128 MiB of HBM per device.

v0:
```python
import jax
import jax.numpy as jnp
from jax import lax
from jax.sharding import PartitionSpec as P

HEADS = 8
STEPS = 50
epsilon = 1e-06
flow_shift = 5.0
highest = lax.Precision.HIGHEST


def from_partner(shard, axis, bit):
    return lax.ppermute(shard, axis, [(i, i ^ 1 << bit) for i in range(lax.axis_size(axis))])


def with_halo(block, sides, width):
    for axis, dim in sides:
        count = lax.axis_size(axis)
        forward = [(i, i + 1) for i in range(count - 1)]
        backward = [(target, source) for source, target in forward]
        low = lax.ppermute(
            lax.slice_in_dim(block, block.shape[dim] - width, None, axis=dim), axis, forward
        )
        high = lax.ppermute(lax.slice_in_dim(block, 0, width, axis=dim), axis, backward)
        block = jnp.concatenate([low, block, high], axis=dim)
    return block


def layer_norm(values):
    centred = values - jnp.mean(values, -1, keepdims=True)
    return centred * lax.rsqrt(jnp.mean(centred * centred, -1, keepdims=True) + epsilon)


def rms_heads(values, gain_vector, head_width):
    shaped = values.reshape(values.shape[0], -1, head_width)
    scaled = (
        shaped * lax.rsqrt(jnp.mean(shaped * shaped, -1, keepdims=True) + epsilon) * gain_vector
    )
    return scaled.reshape(values.shape[0], -1)


def sigma_at(step_value):
    fraction = 1.0 - step_value.astype(jnp.float32) / STEPS
    return flow_shift * fraction / (1.0 + (flow_shift - 1.0) * fraction)


def pick_scale(scale_table, slot_index):
    slots = jnp.arange(scale_table.shape[0], dtype=jnp.int32)
    return jnp.sum(jnp.where(slots == slot_index, scale_table, 0.0))


def attend(queries, image_keys, image_values, text_keys, text_values, image_mask, text_mask, heads):
    head_width = queries.shape[1] // heads
    score_scale = head_width ** (-0.5)
    dims = (((1,), (1,)), ((), ()))

    def one_head(head_index):
        column_start = head_index * head_width
        query_part = lax.dynamic_slice_in_dim(queries, column_start, head_width, 1)
        key_part = lax.dynamic_slice_in_dim(image_keys, column_start, head_width, 1)
        value_part = lax.dynamic_slice_in_dim(image_values, column_start, head_width, 1)
        text_key_part = lax.dynamic_slice_in_dim(text_keys, column_start, head_width, 1)
        text_value_part = lax.dynamic_slice_in_dim(text_values, column_start, head_width, 1)
        image_scores = (
            lax.dot_general(query_part, key_part, dims, preferred_element_type=jnp.float32)
            * score_scale
        )
        text_scores = (
            lax.dot_general(query_part, text_key_part, dims, preferred_element_type=jnp.float32)
            * score_scale
        )
        image_weights = jnp.where(image_mask, jnp.exp(image_scores), 0.0)
        text_weights = jnp.where(text_mask, jnp.exp(text_scores), 0.0)
        denominator = jnp.sum(image_weights, 1, keepdims=True) + jnp.sum(
            text_weights, 1, keepdims=True
        )
        image_weights = (image_weights / denominator).astype(jnp.bfloat16)
        text_weights = (text_weights / denominator).astype(jnp.bfloat16)
        return jnp.dot(image_weights, value_part, preferred_element_type=jnp.float32) + jnp.dot(
            text_weights, text_value_part, preferred_element_type=jnp.float32
        )

    stacked = lax.map(one_head, jnp.arange(heads, dtype=jnp.int32))
    return stacked.transpose(1, 0, 2).reshape(queries.shape[0], -1).astype(jnp.bfloat16)


def conv_rows(above, centre, below, upsample_weight, upsample_bias):
    tap_list = []
    for row_set in (above, centre, below):
        breadth = row_set.shape[1]
        padded = jnp.pad(row_set, ((0, 0), (1, 1), (0, 0)))
        for col_shift in range(3):
            tap_list.append(padded[:, col_shift : col_shift + breadth])
    patches = jnp.concatenate(tap_list, -1)
    flat_patches = patches.reshape(-1, patches.shape[-1])
    product = jnp.dot(flat_patches, upsample_weight, precision=highest).reshape(centre.shape)
    return product + upsample_bias + centre


def per_device(
    coarse_hidden,
    coarse_modulation,
    final_weight,
    coarse_latent,
    step_index,
    guide_index,
    guide_scales,
    upsample_weight,
    upsample_bias,
    embed_weight,
    embed_bias,
    fine_modulation,
    project_weight,
    query_gain,
    key_gain,
    text_keys,
    text_values,
    text_length,
    output_weight,
):
    row_count = coarse_hidden.shape[1]
    row_cells = coarse_hidden.shape[2]
    model_width = coarse_hidden.shape[3]
    channels = final_weight.shape[1]
    head_width = query_gain.shape[0]
    inner = project_weight.shape[1] // 3
    reach = max(row_count // 2, 1)
    branch = lax.axis_index("cfg")
    seq_index = lax.axis_index("seq")
    normed = layer_norm(coarse_hidden[0].astype(jnp.float32))
    modulated = (normed * (1.0 + coarse_modulation[0, 1]) + coarse_modulation[0, 0]).astype(
        jnp.bfloat16
    )
    velocity = jnp.dot(
        modulated.reshape(row_count * row_cells, model_width),
        final_weight,
        preferred_element_type=jnp.float32,
    ).reshape(row_count, row_cells * channels)
    partner = from_partner(velocity, "cfg", 0)
    conditional = jnp.where(branch == 0, velocity, partner)
    unconditional = jnp.where(branch == 0, partner, velocity)
    guidance = pick_scale(guide_scales, guide_index[0])
    guided = unconditional + guidance * (conditional - unconditional)
    stepped = coarse_latent + (sigma_at(step_index[0] + 1) - sigma_at(step_index[0])) * guided

    def embed_rows(grid_rows):
        grid_tokens = grid_rows.reshape(-1, channels).astype(jnp.bfloat16)
        state = jnp.dot(grid_tokens, embed_weight, preferred_element_type=jnp.float32) + embed_bias
        normed_state = (layer_norm(state) * (1.0 + fine_modulation[1]) + fine_modulation[0]).astype(
            jnp.bfloat16
        )
        return (state, normed_state)

    latent_grid = stepped.reshape(row_count, row_cells, channels)
    rim_width = reach + 1
    rimmed = with_halo(latent_grid, (("seq", 0),), rim_width)
    upsampled = jnp.repeat(jnp.repeat(rimmed, 2, 0), 2, 1)
    span = row_count + 2 * reach
    wide_grid = conv_rows(
        upsampled[1 : 1 + 2 * span],
        upsampled[2 : 2 + 2 * span],
        upsampled[3 : 3 + 2 * span],
        upsample_weight,
        upsample_bias,
    )
    grouped = wide_grid.reshape(span, 2, 2 * row_cells, channels)
    fine_grid = lax.dynamic_index_in_dim(
        grouped[reach : reach + row_count], branch, 1, keepdims=False
    )
    fine_state, fine_normed = embed_rows(fine_grid)

    def normed_rows(grid_rows):
        return embed_rows(grid_rows)[1]

    key_normed = lax.map(normed_rows, wide_grid.reshape(span, 4 * row_cells, channels)).reshape(
        -1, model_width
    )
    token_count = fine_normed.shape[0]
    weight_piece = lax.all_gather(project_weight, ("cfg", "seq"), axis=0, tiled=True)
    query_sum = jnp.dot(fine_normed, weight_piece[:, :inner], preferred_element_type=jnp.float32)
    key_sum = jnp.dot(
        key_normed, weight_piece[:, inner : 2 * inner], preferred_element_type=jnp.float32
    )
    value_sum = jnp.dot(
        key_normed, weight_piece[:, 2 * inner :], preferred_element_type=jnp.float32
    )
    queries = rms_heads(query_sum, query_gain, head_width).astype(jnp.bfloat16)
    keys = rms_heads(key_sum, key_gain, head_width).astype(jnp.bfloat16)
    values = value_sum.astype(jnp.bfloat16)
    image_keys, image_values = (keys, values)
    normed_text_keys = rms_heads(text_keys.astype(jnp.float32), key_gain, head_width).astype(
        jnp.bfloat16
    )
    key_count = image_keys.shape[0]
    query_rows = jnp.arange(token_count, dtype=jnp.int32) // (2 * row_cells)
    key_rows = jnp.arange(key_count, dtype=jnp.int32) // (4 * row_cells)
    distance = key_rows[None, :] - query_rows[:, None]
    global_rows = seq_index * row_count + key_rows - reach
    row_valid = (global_rows >= 0) & (global_rows < row_count * lax.axis_size("seq"))
    image_mask = (distance >= 0) & (distance <= 2 * reach) & row_valid[None, :]
    text_mask = (jnp.arange(text_keys.shape[0], dtype=jnp.int32) < text_length[0])[None, :]
    attended = attend(
        queries,
        image_keys,
        image_values,
        normed_text_keys,
        text_values,
        image_mask,
        text_mask,
        HEADS,
    )
    output_part = jnp.dot(
        attended,
        lax.all_gather(output_weight, ("cfg", "seq"), axis=1, tiled=True),
        preferred_element_type=jnp.float32,
    )
    fine_hidden = (fine_state + fine_modulation[2] * output_part).astype(jnp.bfloat16)
    fine_hidden = fine_hidden.reshape(row_count, 1, 2 * row_cells, model_width)
    fine_latent = fine_grid.reshape(row_count, 1, 2 * row_cells * channels)
    return (guided, fine_latent, fine_hidden)


def solution(mesh):
    placed = (
        P("cfg", "seq", None, None),
        P("cfg", None, None),
        P(),
        P("seq", None),
        P(),
        P(),
        P(),
        P(),
        P(),
        P(),
        P(),
        P(),
        P(("cfg", "seq"), None),
        P(),
        P(),
        P(),
        P(),
        P(),
        P(None, ("cfg", "seq")),
    )
    return jax.shard_map(
        per_device,
        mesh=mesh,
        in_specs=placed,
        out_specs=(P("seq", None), P("seq", "cfg", None), P("seq", "cfg", None, None)),
        check_vma=False,
    )
```

profile of v0, /device:TPU:32, one launch (start us, length us, event | category | flops | bytes accessed | tf_op | source)
XLA Modules:
  0.0 862.9 jit_solution(4221278181841568020)
XLA Ops:
  8.0 1.2 convert_reduce_fusion
  9.3 1.3 fusion.43
  11.5 1.4 fusion.47
  13.4 1.6 collective-permute-start
  17.6 1.1 fusion.39
  19.5 1.3 multiply_add_fusion
  20.9 1.9 collective-permute-start.1
  22.9 6.0 collective-permute-start.2
  29.0 1.8 collective-permute-done.2
  34.1 9.6 %while.21 = (s32[]{:T(128)}, bf16[4,256,2048]{2,1,0:T(8,128)(2,1)}, bf16[4,256,32]{2,1,0:T(8,128)(2,1)S(1)}, bf16[32,2048]{1,0:T(8,128)(2,1)S(1)}, f32[2048]{0:T(1024)S(1)}, /*index=5*/f32[3,2048]{1,0:T(4,128)S(1)}, s32[]{:T(128)}) while((s32[]{:T(128)}, bf16[4,256,2048]{2,1,0:T(8,128)(2,1)}, bf16[4,256,32]{2,1,0:T(8,128)(2,1)S(1)}, ...), condition=%wide.region_9.10_spmd, body=%wide.region_6.9_spmd.sunk | while | flops 38799616 | bytes 7603793 | solution.py:176
  35.1 1.5 fusion.93
  37.5 1.5 fusion.93
  39.9 1.4 fusion.93
  42.2 1.4 fusion.93
  45.5 392.8 %all-gather.3.cloned.1.call-done = bf16[2048,3072]{1,0:T(8,128)(2,1)} async-done(((bf16[8,3072]{1,0:T(8,128)(2,1)}), bf16[2048,3072]{1,0:T(8,128)(2,1)}) %all-gather.3.cloned.1.call-update) | async-done | bytes 12582928 | tf_op jit(solution)/shard_map/all_gather | solution.py:180
  438.2 4.6 slice_bitcast_fusion
  442.9 6.5 copy.109
  449.4 10.0 %multiply_reduce_fusion.1 = (f32[1024,8]{0,1:T(8,128)S(1)}, f32[1024,8,128]{0,2,1:T(8,128)}) fusion(bf16[1024,2048,1]{1,0,2:T(8,128)(2,1)} %bitcast.23, bf16[8,128,2048]{2,1,0:T(8,128)(2,1)} %bitcast.120), kind=kOutput, calls=%fused_computation.46 | convolution fusion | flops 4297056256 | bytes 12615680 | tf_op jit(solution)/shard_map/dot_general | solution.py:182
  459.4 3.5 fusion.29
  463.0 1.2 copy.136
  464.1 1.6 reduce_sum.113
  465.9 4.3 multiply_convert_fusion
  471.7 9.4 %fusion.33 = bf16[1024,1024]{1,0:T(8,128)(2,1)} fusion(bf16[1024,2048]{1,0:T(8,128)(2,1)} %bitcast.22, bf16[2048,3072]{1,0:T(8,128)(2,1)} %all-gather.3.cloned.1.call-done), kind=kOutput, calls=%fused_computation.53 | convolution fusion | flops 4296015872 | bytes 10485760 | tf_op jit(solution)/shard_map/dot_general | solution.py:185
  481.0 57.2 %while.22 = (s32[]{:T(128)}, bf16[8,256,128]{1,2,0:T(8,128)(2,1)S(1)}, s32[8]{0:T(128)S(1)}, bf16[256,1024]{1,0:T(8,128)(2,1)}, bf16[1024,1024]{0,1:T(8,128)(2,1...) while((s32[]{:T(128)}, ...), condition=%wide.region_15.16_spmd.clone, body=%wide.region_12.15_spmd.clone.sunk | while | flops 170786816 | bytes 4013791 | solution.py:84
  482.2 1.6 fusion.97
  484.5 1.1 fusion.96
  486.7 1.3 fusion.99
  489.4 1.6 fusion.97
  493.9 1.3 fusion.99
  496.5 1.6 fusion.97
  501.0 1.3 fusion.99
  503.6 1.6 fusion.97
  505.9 1.1 fusion.96
  508.1 1.3 fusion.99
  510.8 1.6 fusion.97
  513.1 1.1 fusion.96
  515.3 1.3 fusion.99
  517.9 1.6 fusion.97
  520.2 1.1 fusion.96
  522.4 1.3 fusion.99
  525.1 1.6 fusion.97
  527.4 1.1 fusion.96
  529.6 1.3 fusion.99
  532.2 1.6 fusion.97
  534.5 1.1 fusion.96
  536.7 1.3 fusion.99
  538.2 313.4 %all-gather.5.cloned.1.call-done = bf16[1024,2048]{0,1:T(8,128)(2,1)} async-done(((bf16[1024,8]{0,1:T(8,128)(2,1)}), bf16[1024,2048]{0,1:T(8,128)(2,1)}) %all-gather.5.cloned.1.call-update) | async-done | bytes 4194320 | tf_op jit(solution)/shard_map/all_gather | solution.py:215
  851.6 4.5 fusion.32
  (169 shorter events, 36.1 us)
Async XLA Ops:
  7.2 5.8 copy-start
  7.2 8.4 copy-start.3
  7.2 8.5 copy-start.10
  7.2 8.5 copy-start.2
  7.2 431.0 %all-gather.3.cloned.1.call-start = ((), (), s32[]{:S(2)}) async-start(), calls=%async_computation | async-start | bytes 12632064 | tf_op jit(solution)/shard_map/all_gather | solution.py:180
  7.9 843.7 %all-gather.5.cloned.1.call-start = ((), (), s32[]{:S(2)}) async-start(), calls=%async_computation.1 | async-start | bytes 4210688 | tf_op jit(solution)/shard_map/all_gather | solution.py:215
  13.4 6.1 collective-permute-start
  15.8 0.8 copy-start.8
  15.8 0.8 copy-start.6
  16.4 3.1 copy-start.7
  20.9 8.1 collective-permute-start.1
  22.9 7.9 collective-permute-start.2
  31.8 1.1 copy-start.5
  31.9 1.1 copy-start.9
  32.5 1.6 copy-start.1
  32.5 1.6 copy-start.4
  471.7 9.4 %copy-start.11 = (bf16[8,256,128]{1,2,0:T(8,128)(2,1)S(1)}, bf16[8,256,128]{1,2,0:T(8,128)(2,1)}, u32[]{:S(2)}) copy-start(bf16[8,256,128]{1,2,0:T(8,128)(2,1)} %custom-call.3) | copy-start | bytes 1572868
Sparse Core Ops, SparseCore 0:
  9.9 428.2 all-gather.2
  440.1 411.4 all-gather.4
where the time goes:
time: 865 us; the launch traced here: 863 us
  waiting for transfers between devices  709 us (82%)
  matrix products  71.9 us (8%)
  other arithmetic  28.6 us (3%)
  local copies, waits for them, and re-layouts  22.7 us (3%)
  between operations  16 us (2%)
  starting transfers between devices  9.62 us (1%)
    all_gather x1, waiting for transfers between devices, per_device(): lax.all_gather(project_weight, ('cfg', 'seq'), axis=0, tiled=True)  393 us
    all_gather x1, waiting for transfers between devices, per_device(): lax.all_gather(output_weight, ('cfg', 'seq'), axis=1, tiled=True)  313 us
  transfers between devices with their start and end apart: 5, of which 4 were waited for; matrix products, arithmetic and copies ran while one was open for 14% of the time, Pallas kernels for 0%

commit v1 on v0

--- a/solution.py
+++ b/solution.py
@@ -177,7 +177,13 @@
         -1, model_width
     )
     token_count = fine_normed.shape[0]
-    weight_piece = lax.all_gather(project_weight, ("cfg", "seq"), axis=0, tiled=True)
+    _report_rounds = lambda v0: jnp.concatenate(
+        lax.all_to_all(
+            jnp.stack(lax.axis_size(("cfg", "seq")) * [v0], axis=0), ("cfg", "seq"), 0, 0
+        ),
+        axis=0,
+    )
+    weight_piece = _report_rounds(project_weight)
     query_sum = jnp.dot(fine_normed, weight_piece[:, :inner], preferred_element_type=jnp.float32)
     key_sum = jnp.dot(
         key_normed, weight_piece[:, inner : 2 * inner], preferred_element_type=jnp.float32

time: 865 us -> 548 us (0.63)
  the two profiles are of different devices: /device:TPU:32 before, /device:TPU:100 now
where the time goes in v1:
time: 548 us; the launch traced here: 546 us
  waiting for transfers between devices  380 us (69%)
  matrix products  68.3 us (12%)
  local copies, waits for them, and re-layouts  30.1 us (5%)
  starting transfers between devices  23.2 us (4%)
  other arithmetic  22.5 us (4%)
  between operations  16 us (3%)
  loops' own time  6.29 us (1%)
    all_to_all x1, waiting for transfers between devices, per_device(): lax.all_to_all(jnp.stack(lax.axis_size(('cfg', 'seq')) * [v0], axis=0), (...  223 us
    all_gather x1, waiting for transfers between devices, per_device(): lax.all_gather(output_weight, ('cfg', 'seq'), axis=1, tiled=True)  127 us
    ppermute x1, waiting for transfers between devices, from_partner(): lax.ppermute(shard, axis, [(i, i ^ 1 << bit) for i in range(lax.axis_size...  27.2 us
    all_to_all x1, starting transfers between devices, per_device(): lax.all_to_all(jnp.stack(lax.axis_size(('cfg', 'seq')) * [v0], axis=0), (...  14.9 us
    dot_general x8, matrix products, one_head(): lax.dot_general(query_part, key_part, dims, preferred_element_type=jnp.fl...  13 us
    dot_general x2, local copies, waits for them, and re-layouts, per_device(): jnp.dot(key_normed, weight_piece[:, inner:2 * inner], preferred_element_t...  11.1 us
  transfers between devices with their start and end apart: 5, of which 5 were waited for; matrix products, arithmetic and copies ran while one was open for 20% of the time, Pallas kernels for 0%

profile of v1, /device:TPU:100, one launch (start us, length us, event | category | flops | bytes accessed | tf_op | source)
XLA Modules:
  0.0 546.3 jit_solution(17606746739691629248)
XLA Ops:
  7.2 6.9 %stack.2 = bf16[256,8,3072]{2,1,0:T(8,128)(2,1)} broadcast(bf16[8,3072]{1,0:T(8,128)(2,1)} %param.35), dimensions={1,2} | broadcast | bytes 12632064 | tf_op jit(solution)/shard_map/stack | solution.py:182
  14.1 14.9 %all-to-all-start = ((bf16[256,8,3072]{2,1,0:T(8,128)(2,1)}), bf16[256,8,3072]{2,1,0:T(8,128)(2,1)}, u32[]{:S(2)}, u32[]{:S(2)}) async-start(bf16[256,8,3072]{2,1,0:T(8,128)(2,1)} %stack.2), calls=%async_computation | async-start | bytes 25165824 | tf_op jit(solution)/shard_map/all_to_all | solution.py:181
  30.5 1.3 collective-permute-start
  34.4 1.1 fusion.39
  36.3 27.2 %collective-permute-done = f32[2,2048]{1,0:T(2,128)S(1)} collective-permute-done((f32[2,2048]{1,0:T(2,128)S(1)}, f32[2,2048]{1,0:T(2,128)S(1)}, u32[]{:S(2)}, u32[]{:S(2)}) %collective-permute-start) | collective-permute-done | bytes 16416 | tf_op jit(solution)/shard_map/ppermute | solution.py:14
  63.5 1.3 multiply_add_fusion
  64.8 1.9 collective-permute-start.1
  66.8 5.1 collective-permute-start.2
  72.0 2.0 collective-permute-done.1
  79.1 9.6 %while.21 = (s32[]{:T(128)}, bf16[4,256,2048]{2,1,0:T(8,128)(2,1)}, bf16[4,256,32]{2,1,0:T(8,128)(2,1)S(1)}, bf16[32,2048]{1,0:T(8,128)(2,1)S(1)}, f32[2048]{0:T(1024)S(1)}, /*index=5*/f32[3,2048]{1,0:T(4,128)S(1)}, s32[]{:T(128)}) while((s32[]{:T(128)}, bf16[4,256,2048]{2,1,0:T(8,128)(2,1)}, bf16[4,256,32]{2,1,0:T(8,128)(2,1)S(1)}, ...), condition=%wide.region_9.10_spmd, body=%wide.region_6.9_spmd.sunk | while | flops 38799616 | bytes 7603293 | solution.py:176
  80.2 1.5 fusion.93
  82.6 1.4 fusion.93
  84.9 1.4 fusion.93
  87.2 1.5 fusion.93
  88.7 223.2 %all-to-all-done = bf16[256,8,3072]{2,1,0:T(8,128)(2,1)} async-done(((bf16[256,8,3072]{2,1,0:T(8,128)(2,1)}), bf16[256,8,3072]{2,1,0:T(8,128)(2,1)}, u32[]{:S(2)}, u32[]{:S(2)}) %all-to-all-start) | async-done | bytes 12582944 | tf_op jit(solution)/shard_map/all_to_all | solution.py:181
  311.9 4.6 slice_bitcast_fusion
  316.5 3.5 fusion.29
  320.1 1.2 copy.136
  321.2 1.6 reduce_sum.113
  323.0 6.5 %copy.109 = bf16[1024,2048]{1,0:T(8,128)(2,1)} copy(bf16[1024,2048]{0,1:T(8,128)(2,1)} %slice_bitcast_fusion) | data formatting | bytes 8388608 | tf_op jit(solution)/shard_map/dot_general | solution.py:188
  329.5 7.8 %multiply_reduce_fusion.1 = (f32[1024,8]{0,1:T(8,128)S(1)}, f32[1024,8,128]{0,2,1:T(8,128)S(1)}) fusion(bf16[1024,2048,1]{1,0,2:T(8,128)(2,1)} %bitcast.141, bf16[8,128,2048]{2,1,0:T(8,128)(2,1)} %bitcast.121), kind=kOutput, calls=%fused_computation.46 | convolution fusion | flops 4297056256 | bytes 12615680 | tf_op jit(solution)/shard_map/dot_general | solution.py:188
  337.4 7.9 %fusion.33 = bf16[1024,1024]{1,0:T(8,128)(2,1)} fusion(bf16[1024,2048]{1,0:T(8,128)(2,1)S(1)} %bitcast.142, bf16[2048,3072]{1,0:T(8,128)(2,1)} %bitcast.20), kind=kOutput, calls=%fused_computation.53 | convolution fusion | flops 4296015872 | bytes 10485760 | tf_op jit(solution)/shard_map/dot_general | solution.py:191
  346.7 2.2 multiply_convert_fusion
  348.9 58.7 %while.22 = (s32[]{:T(128)}, bf16[8,256,128]{1,2,0:T(8,128)(2,1)S(1)}, s32[8]{0:T(128)S(1)}, bf16[256,1024]{1,0:T(8,128)(2,1)}, bf16[1024,1024]{0,1:T(8,128)(2,1...) while((s32[]{:T(128)}, ...), condition=%wide.region_15.16_spmd.clone, body=%wide.region_12.15_spmd.clone.sunk | while | flops 170786816 | bytes 4013799 | solution.py:84
  350.9 1.1 fusion.96
  352.0 1.6 fusion.97
  354.7 1.3 fusion.99
  358.2 1.1 fusion.96
  359.4 1.6 fusion.97
  362.1 1.3 fusion.99
  365.6 1.1 fusion.96
  366.7 1.6 fusion.97
  369.4 1.3 fusion.99
  372.9 1.1 fusion.96
  374.0 1.6 fusion.97
  376.7 1.3 fusion.99
  380.3 1.1 fusion.96
  381.4 1.6 fusion.97
  384.1 1.3 fusion.99
  387.6 1.1 fusion.96
  388.7 1.6 fusion.97
  391.4 1.3 fusion.99
  396.0 1.6 fusion.97
  398.8 1.3 fusion.99
  403.4 1.6 fusion.97
  406.1 1.3 fusion.99
  407.6 127.4 %all-gather.2.cloned.1.call-done = bf16[1024,2048]{0,1:T(8,128)(2,1)} async-done(((bf16[1024,8]{0,1:T(8,128)(2,1)}), bf16[1024,2048]{0,1:T(8,128)(2,1)}) %all-gather.2.cloned.1.call-update) | async-done | bytes 4194320 | tf_op jit(solution)/shard_map/all_gather | solution.py:221
  535.0 4.5 fusion.32
  (177 shorter events, 36.1 us)
Async XLA Ops:
  7.2 22.9 %copy-start = (bf16[2048,32]{0,1:T(8,128)(2,1)S(1)}, bf16[2048,32]{0,1:T(8,128)(2,1)}, u32[]{:S(2)}) copy-start(bf16[2048,32]{0,1:T(8,128)(2,1)} %param.25) | copy-start | bytes 393220
  14.1 14.9 %copy-start.3 = (bf16[1,2,64,2048]{3,2,1,0:T(8,128)(2,1)S(1)}, bf16[1,2,64,2048]{3,2,1,0:T(8,128)(2,1)}, u32[]{:S(2)}) copy-start(bf16[1,2,64,2048]{3,2,1,0:T(8,128)(2,1)} %param.23) | copy-start | bytes 1572868
  14.1 15.6 %copy-start.8 = (f32[1,2,2048]{2,1,0:T(2,128)S(1)}, f32[1,2,2048]{2,1,0:T(2,128)}, u32[]{:S(2)}) copy-start(f32[1,2,2048]{2,1,0:T(2,128)} %param.24) | copy-start | bytes 49156
  14.1 297.8 %all-to-all-start = ((bf16[256,8,3072]{2,1,0:T(8,128)(2,1)}), bf16[256,8,3072]{2,1,0:T(8,128)(2,1)}, u32[]{:S(2)}, u32[]{:S(2)}) async-start(bf16[256,8,3072]{2,1,0:T(8,128)(2,1)} %stack.2), calls=%async_computation | async-start | bytes 25165824 | tf_op jit(solution)/shard_map/all_to_all | solution.py:181
  29.0 3.5 copy-start.4
  29.0 506.0 %all-gather.2.cloned.1.call-start = ((), (), s32[]{:S(2)}) async-start(), calls=%async_computation.1 | async-start | bytes 4210688 | tf_op jit(solution)/shard_map/all_gather | solution.py:221
  30.5 33.0 %collective-permute-start = (f32[2,2048]{1,0:T(2,128)S(1)}, f32[2,2048]{1,0:T(2,128)S(1)}, u32[]{:S(2)}, u32[]{:S(2)}) collective-permute-start(f32[2,2048]{1,0:T(2,128)S(1)} %reshape.240), channel_id=1, source_target_pairs={{0,128},{128,0},{1,129},{129,1},{2,130},{130,2},{3,131},{131,3},{4... | collective-permute-start | bytes 49160 | tf_op jit(solution)/shard_map/ppermute | solution.py:14
  32.6 0.8 copy-start.9
  32.6 1.4 copy-start.13
  32.6 1.4 copy-start.11
  33.2 2.3 copy-start.5
  33.2 30.3 %copy-start.10 = (f32[2,2048]{1,0:T(2,128)S(1)}, f32[2,2048]{1,0:T(2,128)}, u32[]{:S(2)}) copy-start(f32[2,2048]{1,0:T(2,128)} %param.26) | copy-start | bytes 49156
  64.8 9.1 %collective-permute-start.1 = (f32[2,64,32]{2,1,0:T(8,128)S(1)}, f32[2,64,32]{2,1,0:T(8,128)S(1)}, u32[]{:S(2)}, u32[]{:S(2)}) collective-permute-start(f32[2,64,32]{2,1,0:T(8,128)S(1)} %reshape.241), channel_id=1, source_target_pairs={{0,1},{1,2},{2,3},{3,4},{4,5},{5,6},{6,7},{7,8},{8,9},{9,10},{10,1... | collective-permute-start | bytes 49160 | tf_op jit(solution)/shard_map/ppermute | solution.py:22
  66.8 7.2 %collective-permute-start.2 = (f32[2,64,32]{2,1,0:T(8,128)S(1)}, f32[2,64,32]{2,1,0:T(8,128)S(1)}, u32[]{:S(2)}, u32[]{:S(2)}) collective-permute-start(f32[2,64,32]{2,1,0:T(8,128)S(1)} %reshape.241), channel_id=1, source_target_pairs={{1,0},{2,1},{3,2},{4,3},{5,4},{6,5},{7,6},{8,7},{9,8},{10,9},{11,1... | collective-permute-start | bytes 49160 | tf_op jit(solution)/shard_map/ppermute | solution.py:25
  75.0 1.1 copy-start.7
  75.0 1.1 copy-start.12
  75.6 2.5 copy-start.2
  75.6 2.5 copy-start.6
  329.5 7.8 %copy-start.14 = (bf16[4,256,2048]{2,1,0:T(8,128)(2,1)S(1)}, bf16[4,256,2048]{2,1,0:T(8,128)(2,1)}, u32[]{:S(2)}) copy-start(bf16[4,256,2048]{2,1,0:T(8,128)(2,1)} %get-tuple-element.87) | copy-start | bytes 12582916
  346.7 2.2 copy-start.15
  535.0 4.5 copy-start.1
Sparse Core Ops, SparseCore 0:
  31.9 502.9 all-gather.1
